TPU v7x, 32 devices: a whole 2x2x4 slice. The times are simulated.
32 devices in a mesh: ctx: 8 (over z, y), head: 4 (over x, core).
Axes of the slice: x: 2, y: 2, z: 4, core: 2. Of those that a mesh axis runs over, the one named last changes fastest.
Arguments:
- linear_query: bfloat16 [2048, 8192], P('ctx', 'head'), may hold values from -6 to 6
- linear_key: bfloat16 [2048, 8192], P('ctx', 'head'), may hold values from -6 to 6
- linear_value: bfloat16 [2048, 8192], P('ctx', 'head'), may hold values from -6 to 6
- log_decay: float32 [64, 2048], P('head', 'ctx'), may hold values from -1.2 to 0, as said below
- norm_gain: float32 [8192], P('head'), may hold values from 0.25 to 1.75
- soft_query: bfloat16 [2048, 8192], P('ctx', 'head'), may hold values from -4.5 to 4.5
- soft_key: bfloat16 [2048, 8192], P('ctx', 'head'), may hold values from -4.5 to 4.5
- soft_value: bfloat16 [2048, 8192], P('ctx', 'head'), may hold values from -6 to 6
- block_index: int32 [16, 5], P('ctx'), may hold values from 0 to 15, as said below
- block_count: int32 [16], P('ctx'), may hold values from 1 to 5, as said below
Outputs:
- linear_rows: bfloat16 [2048, 8192], P(('ctx', 'head'))
- softmax_rows: bfloat16 [2048, 8192], P(('ctx', 'head'))
Inputs may be any that keep to these rules, and one draw needn't show every extreme that they name: `block_index`: entry 0 of row r is r itself; entries 1 to block_count[r] - 1 are distinct blocks from r - 4 to r - 1, and the farthest of them, r - 4, is named in some row; the entries from block_count[r] on equal r. `block_count`: at most r + 1 for row r; 5 in some row. `log_decay`: strictly negative.
All inputs are finite; a program needn't handle non-finite values.
Results may differ from a plain program's by a relative error of at most 0.0057.
Values may be sent and summed in bfloat16 or wider, within the bound.
A program may use at most 192 MiB of HBM per device.

v0:
```python
import math

import jax
import jax.numpy as jnp
from jax import lax
from jax.sharding import PartitionSpec as P

BLK = 128
WIN_SEC = 2


EPS = 1e-06


def carried_in(value, axis, join, neutral):
    count, mine = (lax.axis_size(axis), lax.axis_index(axis))
    pieces = jax.tree.map(lambda part: lax.all_gather(part, axis), value)
    subtotal = jax.tree.map(
        lambda part, zero: jnp.full_like(part, 0) + jnp.asarray(zero, part.dtype), value, neutral
    )

    def step(position, subtotal):
        longer = join(subtotal, jax.tree.map(lambda part: part[position], pieces))
        return jax.tree.map(lambda new, old: jnp.where(position < mine, new, old), longer, subtotal)

    return lax.fori_loop(0, count - 1, step, subtotal)


def passed_along(block, axis, distance):
    devices = range(lax.axis_size(axis))
    route = [(i - distance, i) for i in devices if i - distance in devices]
    return lax.ppermute(block, axis, route)


def causal_mask(length):
    rows_iota = lax.broadcasted_iota(jnp.int32, (length, length), 0)
    cols_iota = lax.broadcasted_iota(jnp.int32, (length, length), 1)
    return cols_iota <= rows_iota


def to_blocks(matrix, heads):
    length, columns = matrix.shape
    return matrix.reshape(length // BLK, BLK, heads, columns // heads)


def block_state(carried, keys_blk, values_blk, cumul_blk, total_blk):
    factor = jnp.exp(total_blk[:, None] - cumul_blk).T
    decayed = (keys_blk.astype(jnp.float32) * factor[:, :, None]).astype(jnp.bfloat16)
    update = jnp.einsum("jhd,jhe->hde", decayed, values_blk, preferred_element_type=jnp.float32)
    return jnp.exp(total_blk)[:, None, None] * carried + update


def block_output(carried, query_blk, keys_blk, values_blk, cumul_blk):
    scores = jnp.einsum("thd,jhd->htj", query_blk, keys_blk, preferred_element_type=jnp.float32)
    differ = cumul_blk[:, :, None] - cumul_blk[:, None, :]
    allowed = causal_mask(query_blk.shape[0])
    weights = jnp.where(allowed[None], jnp.exp(jnp.minimum(differ, 0.0)), 0.0)
    mixing = (scores * weights).astype(jnp.bfloat16)
    inside = jnp.einsum("htj,jhd->thd", mixing, values_blk, preferred_element_type=jnp.float32)
    decayed_query = (query_blk.astype(jnp.float32) * jnp.exp(cumul_blk).T[:, :, None]).astype(
        jnp.bfloat16
    )
    across = jnp.einsum(
        "thd,hde->the",
        decayed_query,
        carried.astype(jnp.bfloat16),
        preferred_element_type=jnp.float32,
    )
    return inside + across


def combine_states(earlier, later):
    return (earlier[0] * later[0], later[0][:, None, None] * earlier[1] + later[1])


def carry_in(final, section_total):
    identity = (jnp.ones(section_total.shape, jnp.float32), jnp.zeros_like(final))
    result = carried_in((jnp.exp(section_total), final), "ctx", combine_states, identity)
    return result[1]


def linear_layer(linear_query, linear_key, linear_value, log_decay, norm_gain):
    length, columns = linear_query.shape
    heads = log_decay.shape[0]
    width = columns // heads
    blocks_here = length // BLK
    query_blocks = to_blocks(linear_query, heads)
    keys_blocks = to_blocks(linear_key, heads)
    values_blocks = to_blocks(linear_value, heads)
    per_block = log_decay.reshape(heads, blocks_here, BLK).transpose(1, 0, 2)
    cumulative = jnp.cumsum(per_block, axis=2)
    totals = cumulative[:, :, -1]
    section_cum = jnp.cumsum(log_decay, axis=1)
    section_total = section_cum[:, -1]
    start = jnp.zeros((heads, width, width), jnp.float32)

    def advance_both(carried, pieces):
        query_blk, keys_blk, values_blk, cumul_blk, total_blk = pieces
        output = block_output(carried, query_blk, keys_blk, values_blk, cumul_blk)
        return (block_state(carried, keys_blk, values_blk, cumul_blk, total_blk), output)

    final, outputs = lax.scan(
        advance_both, start, (query_blocks, keys_blocks, values_blocks, cumulative, totals)
    )
    incoming = carry_in(final, section_total)
    queries_flat = linear_query.reshape(length, heads, width)
    scaled = (queries_flat.astype(jnp.float32) * jnp.exp(section_cum).T[:, :, None]).astype(
        jnp.bfloat16
    )
    raw = outputs.reshape(length, heads, width) + jnp.einsum(
        "thd,hde->the", scaled, incoming.astype(jnp.bfloat16), preferred_element_type=jnp.float32
    )
    square_mean = jnp.mean(raw * raw, axis=2, keepdims=True)
    normed = raw * lax.rsqrt(square_mean + EPS) * norm_gain.reshape(heads, width)
    return normed.astype(jnp.bfloat16).reshape(length, columns)


def attend(query_blk, keys_sel, values_sel, index_row, count_row, row_global):
    width = query_blk.shape[-1]
    inverse_root = 1.0 / math.sqrt(width)
    scores = (
        jnp.einsum("thd,kjhd->htkj", query_blk, keys_sel, preferred_element_type=jnp.float32)
        * inverse_root
    )
    slot_used = jnp.arange(index_row.shape[0], dtype=jnp.int32) < count_row
    off_diagonal = jnp.logical_not(index_row == row_global)
    allowed = slot_used[None, :, None] & (
        off_diagonal[None, :, None] | causal_mask(query_blk.shape[0])[:, None, :]
    )
    scores = jnp.where(allowed[None], scores, -jnp.inf)
    highest = jnp.max(scores, axis=(2, 3), keepdims=True)
    raised = jnp.exp(scores - highest)
    weights = (raised / jnp.sum(raised, axis=(2, 3), keepdims=True)).astype(jnp.bfloat16)
    output = jnp.einsum("htkj,kjhd->thd", weights, values_sel, preferred_element_type=jnp.float32)
    return output.astype(jnp.bfloat16)


def softmax_layer(soft_query, soft_key, soft_value, block_index, block_count, heads):
    length, columns = soft_query.shape
    per_section = length // BLK
    own_pair = (soft_key, soft_value)
    pieces = []
    for distance in range(WIN_SEC, 0, -1):
        pieces.append(passed_along((own_pair[0], own_pair[1]), "ctx", distance))
    window_key = jnp.concatenate([piece[0] for piece in pieces] + [soft_key], axis=0)
    window_value = jnp.concatenate([piece[1] for piece in pieces] + [soft_value], axis=0)
    key_blocks = to_blocks(window_key, heads)
    value_blocks = to_blocks(window_value, heads)
    section = lax.axis_index("ctx")
    first_block = (section - WIN_SEC) * per_section
    query_blocks = to_blocks(soft_query, heads)
    own_rows = section * per_section + jnp.arange(per_section, dtype=jnp.int32)

    def one_block(inputs):
        query_blk, index_row, count_row, row_global = inputs
        local_row = index_row - first_block
        keys_sel = jnp.take(key_blocks, local_row, axis=0)
        values_sel = jnp.take(value_blocks, local_row, axis=0)
        return attend(query_blk, keys_sel, values_sel, index_row, count_row, row_global)

    outputs = lax.map(one_block, (query_blocks, block_index, block_count, own_rows))
    return outputs.reshape(length, columns)


def local(
    linear_query,
    linear_key,
    linear_value,
    log_decay,
    norm_gain,
    soft_query,
    soft_key,
    soft_value,
    block_index,
    block_count,
):
    heads = log_decay.shape[0]
    linear_heads = linear_layer(linear_query, linear_key, linear_value, log_decay, norm_gain)
    softmax_heads = softmax_layer(soft_query, soft_key, soft_value, block_index, block_count, heads)
    result = (
        lax.all_to_all(linear_heads, "head", split_axis=0, concat_axis=1, tiled=True),
        lax.all_to_all(softmax_heads, "head", split_axis=0, concat_axis=1, tiled=True),
    )
    return (result[0], result[1])


def solution(mesh):
    in_specs = (
        P("ctx", "head"),
        P("ctx", "head"),
        P("ctx", "head"),
        P("head", "ctx"),
        P("head"),
        P("ctx", "head"),
        P("ctx", "head"),
        P("ctx", "head"),
        P("ctx", None),
        P("ctx"),
    )
    out_specs = (P(("ctx", "head"), None), P(("ctx", "head"), None))
    return jax.shard_map(local, mesh=mesh, in_specs=in_specs, out_specs=out_specs, check_vma=False)
```

profile of v0, /device:TPU:0, one launch (start us, length us, event | category | flops | bytes accessed | tf_op | source)
XLA Modules:
  0.0 395.8 jit_solution(15640829130528130471)
XLA Ops:
  8.6 2.4 copy.104
  11.1 1.4 copy.105
  13.7 70.7 %while.38 = (s32[]{:T(128)}, f32[16,128,128]{2,1,0:T(8,128)S(1)}, f32[2,128,16,128]{1,0,3,2:T(2,128)}, f32[2,16]{1,0:T(2,128)S(1)}, bf16[2,128,16,128]{3,2,1,0:T...) while((s32[]{:T(128)}, f32[16,128,128]{2,1,0:T(8,128)S(1)}, ...), condition=%wide.region_2.3_spmd.clone, body=%wide.region_1.2_spmd.clone.sunk | while | flops 272648192 | bytes 25264664 | solution.py:102
  13.7 1.6 constant_dynamic-slice_fusion.11
  16.5 1.9 convolution_bitcast_fusion.3
  18.4 1.9 fusion.61
  20.3 26.6 %dynamic_update_slice.13 = f32[2,128,16,128]{1,0,3,2:T(2,128)} dynamic-update-slice(f32[2,128,16,128]{1,0,3,2:T(2,128)} %get-tuple-element.512, f32[1,128,16,128]{1,0,3,2:T(1,128)S(1)} %bitcast.182, s32[]{:T(128)} %get-tuple-element.510, s32[]{:T(128)} %constant.86.clone.1..sunk, s32[]{:T(128)} %constant.86.clone.1..sunk, s32[]{:T(128)} %constant.86.clone.1..sunk) | dynamic-update-slice | bytes 2097156 | tf_op jit(solution)/shard_map/while/body/jit(dynamic_update_index_in_dim)/dynamic_update_slice | solution.py:102
  47.0 2.0 convolution_add_fusion.2
  49.1 1.6 constant_dynamic-slice_fusion.11
  51.8 1.9 convolution_bitcast_fusion.3
  53.8 1.9 fusion.61
  55.7 26.6 %dynamic_update_slice.13 = f32[2,128,16,128]{1,0,3,2:T(2,128)} dynamic-update-slice(f32[2,128,16,128]{1,0,3,2:T(2,128)} %get-tuple-element.512, f32[1,128,16,128]{1,0,3,2:T(1,128)S(1)} %bitcast.182, s32[]{:T(128)} %get-tuple-element.510, s32[]{:T(128)} %constant.86.clone.1..sunk, s32[]{:T(128)} %constant.86.clone.1..sunk, s32[]{:T(128)} %constant.86.clone.1..sunk) | dynamic-update-slice | bytes 2097156 | tf_op jit(solution)/shard_map/while/body/jit(dynamic_update_index_in_dim)/dynamic_update_slice | solution.py:102
  82.4 2.0 convolution_add_fusion.2
  85.4 6.0 %collective-permute-start = (bf16[256,2048]{1,0:T(8,128)(2,1)}, bf16[256,2048]{1,0:T(8,128)(2,1)}, u32[]{:S(2)}, u32[]{:S(2)}) collective-permute-start(bf16[256,2048]{1,0:T(8,128)(2,1)} %param.25), channel_id=1, source_target_pairs={{0,8},{4,12},{8,16},{12,20},{16,24},{20,28},{1,9},{5,13},{9,17},{1... | collective-permute-start | bytes 3145736 | tf_op jit(solution)/shard_map/ppermute | solution.py:32
  91.4 4.4 %collective-permute-start.1 = (bf16[256,2048]{1,0:T(8,128)(2,1)}, bf16[256,2048]{1,0:T(8,128)(2,1)}, u32[]{:S(2)}, u32[]{:S(2)}) collective-permute-start(bf16[256,2048]{1,0:T(8,128)(2,1)} %param.25), channel_id=1, source_target_pairs={{0,4},{4,8},{8,12},{12,16},{16,20},{20,24},{24,28},{1,5},{5,9},{9,... | collective-permute-start | bytes 3145736 | tf_op jit(solution)/shard_map/ppermute | solution.py:32
  95.8 1.5 collective-permute-start.2
  97.4 4.4 %collective-permute-start.3 = (bf16[256,2048]{1,0:T(8,128)(2,1)}, bf16[256,2048]{1,0:T(8,128)(2,1)}, u32[]{:S(2)}, u32[]{:S(2)}) collective-permute-start(bf16[256,2048]{1,0:T(8,128)(2,1)} %param.24), channel_id=1, source_target_pairs={{0,4},{4,8},{8,12},{12,16},{16,20},{20,24},{24,28},{1,5},{5,9},{9,... | collective-permute-start | bytes 3145736 | tf_op jit(solution)/shard_map/ppermute | solution.py:32
  104.4 188.7 %all-reduce = f32[128]{0:T(128)S(1)} all-reduce(f32[128]{0:T(128)S(1)} %dynamic-update-slice), channel_id=2, replica_groups=mesh['ctx'=8,'head'=4] {'ctx'}, use_global_device_ids=true, to_apply=%add | all-reduce | flops 128 | bytes 1024
  293.2 4.0 %reshape.126 = f32[256,16,128]{0,2,1:T(8,128)} reshape(f32[2,128,16,128]{1,0,3,2:T(2,128)} %get-tuple-element.187) | data formatting | bytes 4194304 | tf_op jit(solution)/shard_map/reshape | solution.py:110
  297.2 1.2 copy.108
  298.6 1.7 maximum_bitcast_fusion
  300.3 2.7 copy.107
  303.1 1.4 maximum_bitcast_fusion.1
  304.5 2.8 copy.109
  307.3 40.2 %while.37 = (s32[]{:T(128)}, bf16[2,128,16,128]{3,2,1,0:T(8,128)(2,1)}, s32[2,5]{1,0:T(2,128)S(1)}, s32[]{:T(128)}, bf16[6,128,16,128]{3,2,1,0:T(8,128)(2,1)}, /...) while((s32[]{:T(128)}, ...), condition=%wide.region_11.13_spmd, body=%wide.region_8.12_spmd.sunk | while | flops 689878016 | bytes 69611904 | solution.py:161
  307.3 2.9 gather_fusion
  310.2 4.4 %gather_fusion.1 = bf16[5,128,16,128]{3,2,1,0:T(8,128)(2,1)} fusion(bf16[6,128,16,128]{3,2,1,0:T(8,128)(2,1)} %get-tuple-element.579, s32[1024]{0:T(1024)S(1)} %pad_clamp_fusion.2), kind=kCustom, calls=%fused_computation.1.clone.clone.1 | custom fusion | bytes 5242900 | tf_op jit(solution)/shard_map/while/body/eval_jaxpr/jit(_take)/gather | solution.py:157
  314.6 2.3 broadcast_select_fusion.3
  323.2 2.6 fusion.59
  327.4 2.9 gather_fusion
  330.4 4.4 %gather_fusion.1 = bf16[5,128,16,128]{3,2,1,0:T(8,128)(2,1)} fusion(bf16[6,128,16,128]{3,2,1,0:T(8,128)(2,1)} %get-tuple-element.579, s32[1024]{0:T(1024)S(1)} %pad_clamp_fusion.2), kind=kCustom, calls=%fused_computation.1.clone.clone.1 | custom fusion | bytes 5242900 | tf_op jit(solution)/shard_map/while/body/eval_jaxpr/jit(_take)/gather | solution.py:157
  334.7 2.3 broadcast_select_fusion.3
  343.3 2.6 fusion.59
  347.5 2.4 all_to_all.32
  349.9 4.3 %all-to-all-start.1 = ((bf16[4,64,2048]{2,1,0:T(8,128)(2,1)}), bf16[4,64,2048]{2,1,0:T(8,128)(2,1)}, u32[]{:S(2)}, u32[]{:S(2)}) async-start(bf16[4,64,2048]{2,1,0:T(8,128)(2,1)} %all_to_all.32), calls=%async_computation.1 | async-start | bytes 2097152 | tf_op jit(solution)/shard_map/all_to_all | solution.py:182
  354.2 10.6 %while.39 = (s32[]{:T(128)}, f32[16,128,128]{2,1,0:T(8,128)S(1)}, s32[]{:T(128)}, f32[8,16]{1,0:T(8,128)S(1)}, f32[8,16,128,128]{3,2,1,0:T(8,128)}, /*index=5*/s32[]{:T(128)}, s32[]{:T(128)}) while((s32[]{:T(128)}, f32[16,128,128]{2,1,0:T(8,128)S(1)}, s32[]{:T(128)}, f32[8,16]{1,0:T(8,128)S(1)}, f32[8,16,128,128]{3,2,1,0:T(8,128)}, ...), condition=%wide.region_6.7_spmd.clone, body=%wide.region_5.6_spmd.clone.sunk | while | flops 1048580 | bytes 3146025 | solution.py:26
  354.3 1.6 fusion.62
  355.9 1.5 fusion.62
  357.4 1.5 fusion.62
  358.9 1.5 fusion.62
  360.4 1.5 fusion.62
  361.9 1.5 fusion.62
  363.4 1.5 fusion.62
  364.9 2.3 multiply_reduce_fusion
  368.7 1.3 all_to_all.28
  369.9 3.5 all-to-all-start
  373.5 2.3 copy.103
  375.8 12.1 %all-to-all-done = bf16[4,64,2048]{2,1,0:T(8,128)(2,1)S(1)} async-done(((bf16[4,64,2048]{2,1,0:T(8,128)(2,1)}), bf16[4,64,2048]{2,1,0:T(8,128)(2,1)S(1)}, u32[]{:S(2)}, u32[]{:S(2)}) %all-to-all-start) | async-done | bytes 1048608 | tf_op jit(solution)/shard_map/all_to_all | solution.py:181
  (129 shorter events, 26.2 us)
Async XLA Ops:
  7.2 0.7 copy-start
  7.2 5.3 %copy-start.9 = (bf16[256,2048]{1,0:T(8,128)(2,1)S(1)}, bf16[256,2048]{1,0:T(8,128)(2,1)}, u32[]{:S(2)}) copy-start(bf16[256,2048]{1,0:T(8,128)(2,1)} %param.18) | copy-start | bytes 3145732
  7.2 347.0 %all-gather.4.cloned.1.call-start = ((), (), s32[]{:S(2)}) async-start(), calls=%async_computation.2 | async-start | bytes 9437184 | tf_op jit(solution)/shard_map/all_gather | solution.py:17
  13.7 88.8 %copy-start.18 = (u32[32]{0:T(128)S(1)}, u32[32]{0:T(128)}, u32[]{:S(2)}) copy-start(u32[32]{0:T(128)} %constant.99) | copy-start | bytes 388
  13.7 1.6 copy-start.5
  16.5 1.9 copy-start.3
  47.0 2.1 copy-start.6
  49.1 1.6 copy-start.5
  51.8 1.9 copy-start.3
  82.3 2.1 copy-start.6
  84.4 1.0 copy-start.2
  84.4 212.8 %copy-start.10 = (bf16[256,2048]{1,0:T(8,128)(2,1)S(1)}, bf16[256,2048]{1,0:T(8,128)(2,1)}, u32[]{:S(2)}) copy-start(bf16[256,2048]{1,0:T(8,128)(2,1)} %param.23) | copy-start | bytes 3145732
  85.4 213.1 %collective-permute-start = (bf16[256,2048]{1,0:T(8,128)(2,1)}, bf16[256,2048]{1,0:T(8,128)(2,1)}, u32[]{:S(2)}, u32[]{:S(2)}) collective-permute-start(bf16[256,2048]{1,0:T(8,128)(2,1)} %param.25), channel_id=1, source_target_pairs={{0,8},{4,12},{8,16},{12,20},{16,24},{20,28},{1,9},{5,13},{9,17},{1... | collective-permute-start | bytes 3145736 | tf_op jit(solution)/shard_map/ppermute | solution.py:32
  91.4 207.1 %collective-permute-start.1 = (bf16[256,2048]{1,0:T(8,128)(2,1)}, bf16[256,2048]{1,0:T(8,128)(2,1)}, u32[]{:S(2)}, u32[]{:S(2)}) collective-permute-start(bf16[256,2048]{1,0:T(8,128)(2,1)} %param.25), channel_id=1, source_target_pairs={{0,4},{4,8},{8,12},{12,16},{16,20},{20,24},{24,28},{1,5},{5,9},{9,... | collective-permute-start | bytes 3145736 | tf_op jit(solution)/shard_map/ppermute | solution.py:32
  95.8 207.2 %collective-permute-start.2 = (bf16[256,2048]{1,0:T(8,128)(2,1)}, bf16[256,2048]{1,0:T(8,128)(2,1)S(1)}, u32[]{:S(2)}, u32[]{:S(2)}) collective-permute-start(bf16[256,2048]{1,0:T(8,128)(2,1)} %param.24), channel_id=1, source_target_pairs={{0,8},{4,12},{8,16},{12,20},{16,24},{20,28},{1,9},{5,13},{9,17},{1... | collective-permute-start | bytes 3145736 | tf_op jit(solution)/shard_map/ppermute | solution.py:32
  97.4 205.7 %collective-permute-start.3 = (bf16[256,2048]{1,0:T(8,128)(2,1)}, bf16[256,2048]{1,0:T(8,128)(2,1)}, u32[]{:S(2)}, u32[]{:S(2)}) collective-permute-start(bf16[256,2048]{1,0:T(8,128)(2,1)} %param.24), channel_id=1, source_target_pairs={{0,4},{4,8},{8,12},{12,16},{16,20},{20,24},{24,28},{1,5},{5,9},{9,... | collective-permute-start | bytes 3145736 | tf_op jit(solution)/shard_map/ppermute | solution.py:32
  293.2 5.3 %copy-start.13 = (bf16[256,2048]{1,0:T(8,128)(2,1)S(1)}, bf16[256,2048]{1,0:T(8,128)(2,1)}, u32[]{:S(2)}) copy-start(bf16[256,2048]{1,0:T(8,128)(2,1)} %param.25) | copy-start | bytes 3145732
  300.3 2.8 copy-start.14
  304.5 2.8 copy-start.15
  304.5 2.8 copy-start.17
  316.9 1.2 copy-start.7
  323.2 3.1 copy-start.11
  326.4 1.0 copy-start.12
  337.0 1.2 copy-start.7
  343.3 3.1 copy-start.11
  346.5 1.0 copy-start.12
  347.5 6.7 %copy-start.4 = (f32[16,128,128]{2,1,0:T(8,128)S(1)}, f32[16,128,128]{2,1,0:T(8,128)}, u32[]{:S(2)}) copy-start(f32[16,128,128]{2,1,0:T(8,128)} %custom-call.1) | copy-start | bytes 3145732
  349.9 20.0 %all-to-all-start.1 = ((bf16[4,64,2048]{2,1,0:T(8,128)(2,1)}), bf16[4,64,2048]{2,1,0:T(8,128)(2,1)}, u32[]{:S(2)}, u32[]{:S(2)}) async-start(bf16[4,64,2048]{2,1,0:T(8,128)(2,1)} %all_to_all.32), calls=%async_computation.1 | async-start | bytes 2097152 | tf_op jit(solution)/shard_map/all_to_all | solution.py:182
  354.2 10.6 %copy-start.8 = (f32[256,16,128]{0,2,1:T(8,128)S(1)}, f32[256,16,128]{0,2,1:T(8,128)}, u32[]{:S(2)}) copy-start(f32[256,16,128]{0,2,1:T(8,128)} %reshape.126) | copy-start | bytes 6291460
  364.9 2.3 copy-start.16
  368.7 20.3 %copy-start.1 = (f32[16,256]{1,0:T(8,128)S(1)}, f32[16,256]{1,0:T(8,128)}, u32[]{:S(2)}) copy-start(f32[16,256]{1,0:T(8,128)} %param.21) | copy-start | bytes 49156
  369.9 18.0 %all-to-all-start = ((bf16[4,64,2048]{2,1,0:T(8,128)(2,1)}), bf16[4,64,2048]{2,1,0:T(8,128)(2,1)S(1)}, u32[]{:S(2)}, u32[]{:S(2)}) async-start(bf16[4,64,2048]{2,1,0:T(8,128)(2,1)} %all_to_all.28), calls=%async_computation | async-start | bytes 2097152 | tf_op jit(solution)/shard_map/all_to_all | solution.py:181
Sparse Core Ops, SparseCore 0:
  85.5 161.6 all-gather.3
where the time goes:
time: 401 us; the launch traced here: 396 us
  blocking collectives  189 us (47%)
  local copies, waits for them, and re-layouts  108 us (27%)
  other arithmetic  25.9 us (6%)
  starting transfers between devices  24.2 us (6%)
  matrix products  21 us (5%)
  between operations  15 us (4%)
  waiting for transfers between devices  12.2 us (3%)
    unnamed x1, blocking collectives  189 us
    dynamic_update_slice x2, local copies, waits for them, and re-layouts, linear_layer(): lax.scan(advance_both, start, (query_blocks, keys_blocks, values_blocks,...  53.2 us
    ppermute x4, starting transfers between devices, passed_along(): return lax.ppermute(block, axis, route)  16.4 us
    unnamed x35, local copies, waits for them, and re-layouts  14.4 us
    all_to_all x1, waiting for transfers between devices, local(): lax.all_to_all(linear_heads, 'head', split_axis=0, concat_axis=1, tiled=T...  12.1 us
    select_n x7, other arithmetic, step(): jnp.where(position < mine, new, old)  10.3 us
    gather x2, local copies, waits for them, and re-layouts, one_block(): keys_sel = jnp.take(key_blocks, local_row, axis=0)  8.77 us
  transfers between devices with their start and end apart: 7, of which 1 were waited for; matrix products, arithmetic and copies ran while one was open for 18% of the time, Pallas kernels for 0%

commit v1 on v0

v1 whole, which is shorter than its diff:
```python
import functools
import math

import jax
import jax.numpy as jnp
from jax import lax
from jax.experimental import pallas as pl
from jax.experimental.pallas import tpu as pltpu
from jax.sharding import PartitionSpec as P

BLK = 128
HD = 128
REACH = 4
PER_GROUP = 2
EPS = 1e-06
OFF = -1e30
F32 = jnp.float32
BF16 = jnp.bfloat16
MESH = pl.DeviceIdType.MESH
NT = (((1,), (1,)), ((), ()))
TN = (((0,), (0,)), ((), ()))


def dot(a, b):
    return jnp.dot(a, b, preferred_element_type=F32)


def kernel(sections, peers, heads,
           lq, lk, lv, ld, gain, sq, sk, sv, bias,
           out_lin, out_soft,
           ak, av, bk, bv, lstage, sstage, cc, g0s, g1s, exd, exp_, l1, fown, fsend, frecv, xsend, xrecv, inc,
           a_send, a_recv, b_send, b_recv, d_send, d_recv, f_send, f_recv, x_send, x_recv, o_send, o_recv, o_local):
    groups = heads // PER_GROUP
    wide = PER_GROUP * HD
    length = lq.shape[0]
    rows = length // peers
    c, h = lax.axis_index("ctx"), lax.axis_index("head")
    odd = lax.rem(c, 2)
    even = 1 - odd
    partner = c + 1 - 2 * odd
    after, before = lax.rem(c + 2, sections), lax.rem(c + sections - 2, sections)
    has_after, has_before = c + 2 < sections, c >= 2
    has_b = c >= 1
    sends_b = jnp.logical_or(odd == 0, has_before)

    def cols(g):
        return pl.ds(pl.multiple_of(g * wide, wide), wide)

    def hcols(i):
        return pl.ds(pl.multiple_of(i * HD, HD), HD)

    def remote(src, dst, send, recv, where):
        return pltpu.make_async_remote_copy(
            src_ref=src, dst_ref=dst, send_sem=send, recv_sem=recv, device_id=where, device_id_type=MESH)

    def copies_a(g):
        return [remote(src.at[:, cols(g)], dst.at[:, cols(g)], a_send.at[n, g], a_recv.at[n, g], {"ctx": after})
                for n, (src, dst) in enumerate(((sk, ak), (sv, av)))]

    def copies_b(g, sources):
        return [remote(src.at[:, cols(g)], dst.at[:, cols(g)], b_send.at[n, g], b_recv.at[n, g], {"ctx": partner})
                for n, (src, dst) in enumerate(zip(sources, (bk, bv)))]

    def hd(g):
        return pl.ds(g * PER_GROUP, PER_GROUP)

    def copy_f(g):
        return remote(fsend.at[hd(g)], frecv.at[hd(g)], f_send.at[g], f_recv.at[g], {"ctx": partner})

    def copy_x(g):
        return remote(xsend.at[hd(g)], xrecv.at[hd(g)], x_send.at[g], x_recv.at[g], {"ctx": after})

    copy_d = remote(exd, exp_, d_send, d_recv, {"ctx": partner})

    def out_cols(g):
        return pl.ds(pl.multiple_of(h * (heads * HD) + g * wide, wide), wide)

    def copies_out(n, stage, out, g):
        made = []
        for k in range(1, peers):
            to = lax.rem(h + k, peers)
            made.append(remote(stage.at[pl.ds(pl.multiple_of(to * rows, rows), rows), cols(g)],
                               out.at[:, out_cols(g)],
                               o_send.at[n, g, k - 1], o_recv.at[n, g, k - 1], {"head": to}))
        return made

    def copy_local(n, stage, out, g):
        return pltpu.make_async_copy(stage.at[pl.ds(pl.multiple_of(h * rows, rows), rows), cols(g)],
                                     out.at[:, out_cols(g)], o_local.at[n, g])

    barrier = pltpu.get_barrier_semaphore()
    pl.semaphore_signal(barrier, inc=1, device_id={"ctx": partner}, device_id_type=MESH)
    for k in range(1, peers):
        pl.semaphore_signal(barrier, inc=1, device_id={"head": lax.rem(h + k, peers)}, device_id_type=MESH)

    @pl.when(has_after)
    def _():
        pl.semaphore_signal(barrier, inc=1, device_id={"ctx": after}, device_id_type=MESH)

    @pl.when(has_before)
    def _():
        pl.semaphore_signal(barrier, inc=1, device_id={"ctx": before}, device_id_type=MESH)

    pl.semaphore_wait(barrier, peers + has_after.astype(jnp.int32) + has_before.astype(jnp.int32))

    def start_kv(g, carry):
        @pl.when(has_after)
        def _():
            for copy in copies_a(g):
                copy.start()

        @pl.when(odd == 0)
        def _():
            for copy in copies_b(g, (sk, sv)):
                copy.start()
        return carry

    lax.fori_loop(0, groups, start_kv, 0)

    lane = lax.broadcasted_iota(jnp.int32, (heads, length), 1)
    total = ld[...]
    for shift in (1, 2, 4, 8, 16, 32, 64):
        total = total + jnp.where(lax.rem(lane, BLK) >= shift, pltpu.roll(total, shift, 1), 0.0)
    first = jnp.broadcast_to(total[:, BLK - 1:BLK], (heads, HD))
    second = jnp.broadcast_to(total[:, 2 * BLK - 1:2 * BLK], (heads, HD))
    whole = jnp.exp(first + second)
    for i in range(heads):
        cc[i] = total[i:i + 1]
        g0s[i] = first[i:i + 1]
        g1s[i] = second[i:i + 1]
        exd[i] = jnp.broadcast_to(whole[i:i + 1], (8, HD))
    copy_d.start()

    def columns_of(i, b):
        along = jnp.broadcast_to(cc[i, :, pl.ds(b * BLK, BLK)], (BLK, BLK))
        return along, along.T

    def states(g, carry):
        for n in range(PER_GROUP):
            i = g * PER_GROUP + n
            ends = (g0s[i], g1s[i])
            update = []
            for b in range(2):
                along, down = columns_of(i, b)
                part = pl.ds(b * BLK, BLK)
                kc = (lk[part, hcols(i)].astype(F32) * jnp.exp(ends[b] - down)).astype(BF16)
                update.append(lax.dot_general(kc, lv[part, hcols(i)], TN, preferred_element_type=F32))
            final = jnp.exp(ends[1]) * update[0] + update[1]
            l1[i] = update[0].astype(BF16)
            fown[i] = final
            fsend[i] = final.astype(BF16)
        copy_f(g).start()
        return carry

    lax.fori_loop(0, groups, states, 0)

    @pl.when(c < 2)
    def _():
        ak[...] = jnp.zeros_like(ak)
        av[...] = jnp.zeros_like(av)
        xrecv[...] = jnp.zeros_like(xrecv)

    @pl.when(c < 1)
    def _():
        bk[...] = jnp.zeros_like(bk)
        bv[...] = jnp.zeros_like(bv)

    copy_d.wait()
    r_iota = lax.broadcasted_iota(jnp.int32, (BLK, BLK), 0)
    c_iota = lax.broadcasted_iota(jnp.int32, (BLK, BLK), 1)
    scale = 1.0 / math.sqrt(HD)

    def forward(g):
        @pl.when(has_before)
        def _():
            for copy in copies_a(g):
                copy.wait_recv()

        @pl.when(jnp.logical_and(odd == 1, has_before))
        def _():
            for copy in copies_b(g, (ak, av)):
                copy.start()

    def chain(g):
        copy_f(g).wait_recv()

        @pl.when(has_before)
        def _():
            copy_x(g).wait_recv()

        for n in range(PER_GROUP):
            i = g * PER_GROUP + n
            mine, other, x = fown[i], frecv[i].astype(F32), xrecv[i].astype(F32)
            d_mine, d_other = exd[i][:1], exp_[i][:1]
            is_odd = odd == 1
            mid = jnp.where(is_odd, d_other, d_mine) * x + jnp.where(is_odd, other, mine)
            xsend[i] = (jnp.where(is_odd, d_mine, d_other) * mid + jnp.where(is_odd, mine, other)).astype(xsend.dtype)
            inc[i] = jnp.where(is_odd, mid, x).astype(BF16)

        @pl.when(has_after)
        def _():
            copy_x(g).start()

    def softmax(g):
        @pl.when(has_b)
        def _():
            for copy in copies_b(g, (sk, sv)):
                copy.wait_recv()

        causal = c_iota <= r_iota
        for n in range(PER_GROUP):
            i = g * PER_GROUP + n
            kw = jnp.concatenate([ak[:, hcols(i)], bk[:, hcols(i)], sk[:, hcols(i)]], axis=0)
            vw = jnp.concatenate([av[:, hcols(i)], bv[:, hcols(i)], sv[:, hcols(i)]], axis=0)
            for b in range(2):
                part = pl.ds(b * BLK, BLK)
                span = slice(b * BLK, b * BLK + (REACH + 1) * BLK)
                s = lax.dot_general(sq[part, hcols(i)], kw[span], NT, preferred_element_type=F32) * scale
                s = jnp.concatenate([s[:, :REACH * BLK] + bias[b:b + 1, :],
                                     jnp.where(causal, s[:, REACH * BLK:], OFF)], axis=1)
                p = jnp.exp(s - jnp.max(s, axis=1, keepdims=True))
                w = (p * (1.0 / jnp.sum(p, axis=1, keepdims=True))).astype(BF16)
                sstage[part, hcols(i)] = dot(w, vw[span]).astype(BF16)
        for copy in copies_out(1, sstage, out_soft, g):
            copy.start()
        copy_local(1, sstage, out_soft, g).start()

    def linear(g):
        causal = c_iota <= r_iota
        for n in range(PER_GROUP):
            i = g * PER_GROUP + n
            incoming = inc[i]
            for b in range(2):
                part = pl.ds(b * BLK, BLK)
                along, down = columns_of(i, b)
                q, k, v = lq[part, hcols(i)], lk[part, hcols(i)], lv[part, hcols(i)]
                s = lax.dot_general(q, k, NT, preferred_element_type=F32)
                s = s * jnp.where(causal, jnp.exp(jnp.minimum(down - along, 0.0)), 0.0)
                raw = dot(s.astype(BF16), v)
                wide_q = q.astype(F32)
                if b == 0:
                    raw += dot((wide_q * jnp.exp(down)).astype(BF16), incoming)
                else:
                    raw += dot((wide_q * jnp.exp(down)).astype(BF16), l1[i])
                    raw += dot((wide_q * jnp.exp(down + g0s[i])).astype(BF16), incoming)
                square = jnp.mean(raw * raw, axis=1, keepdims=True)
                lstage[part, hcols(i)] = (raw * lax.rsqrt(square + EPS) * gain[:, hcols(i)]).astype(BF16)
        for copy in copies_out(0, lstage, out_lin, g):
            copy.start()
        copy_local(0, lstage, out_lin, g).start()

    forward(0)

    def main(g, carry):
        chain(g)

        @pl.when(g + 1 < groups)
        def _():
            forward(g + 1)
        softmax(g)
        linear(g)
        return carry

    lax.fori_loop(0, groups, main, 0)

    def finish(g, carry):
        @pl.when(has_after)
        def _():
            for copy in copies_a(g):
                copy.wait_send()
            copy_x(g).wait_send()

        @pl.when(sends_b)
        def _():
            for copy in copies_b(g, (sk, sv)):
                copy.wait_send()
        copy_f(g).wait_send()
        for n, (stage, out) in enumerate(((lstage, out_lin), (sstage, out_soft))):
            copy_local(n, stage, out, g).wait()
            for copy in copies_out(n, stage, out, g):
                copy.wait()
        return carry

    lax.fori_loop(0, groups, finish, 0)


def local(sections, peers, linear_query, linear_key, linear_value, log_decay, norm_gain,
          soft_query, soft_key, soft_value, block_index, block_count):
    heads, length = log_decay.shape
    width = linear_query.shape[1]
    groups = heads // PER_GROUP
    here = length // BLK
    own = lax.axis_index("ctx") * here + jnp.arange(here, dtype=jnp.int32)
    named = own[:, None] - REACH + jnp.arange(REACH, dtype=jnp.int32)[None, :]
    used = jnp.arange(block_index.shape[1], dtype=jnp.int32)[None, :] < block_count[:, None]
    seen = jnp.any(used[:, None, :] & (block_index[:, None, :] == named[:, :, None]), axis=2)
    bias = jnp.repeat(jnp.where(seen, 0.0, OFF).astype(F32), BLK, axis=1)
    carried = BF16 if sections <= 8 else F32
    vmem = pl.BlockSpec(memory_space=pltpu.VMEM)
    rows = length // peers
    state = (heads, HD, HD)
    dma = pltpu.SemaphoreType.DMA
    return pl.pallas_call(
        functools.partial(kernel, sections, peers, heads),
        out_shape=[jax.ShapeDtypeStruct((rows, width * peers), BF16)] * 2,
        in_specs=[vmem] * 9,
        out_specs=[pl.BlockSpec(memory_space=pl.ANY)] * 2,
        scratch_shapes=[pltpu.VMEM((length, width), BF16)] * 6 + [
            pltpu.VMEM((heads, 1, length), F32),
            pltpu.VMEM((heads, 1, HD), F32),
            pltpu.VMEM((heads, 1, HD), F32),
            pltpu.VMEM((heads, 8, HD), F32),
            pltpu.VMEM((heads, 8, HD), F32),
            pltpu.VMEM(state, BF16),
            pltpu.VMEM(state, F32),
            pltpu.VMEM(state, BF16),
            pltpu.VMEM(state, BF16),
            pltpu.VMEM(state, carried),
            pltpu.VMEM(state, carried),
            pltpu.VMEM(state, BF16),
            dma((2, groups)), dma((2, groups)), dma((2, groups)), dma((2, groups)),
            dma, dma, dma((groups,)), dma((groups,)), dma((groups,)), dma((groups,)),
            dma((2, groups, peers - 1)), dma((2, groups, peers - 1)), dma((2, groups)),
        ],
        compiler_params=pltpu.CompilerParams(
            collective_id=0, has_side_effects=True, vmem_limit_bytes=48 * 1024 * 1024),
        cost_estimate=pl.CostEstimate(flops=2_400_000_000, bytes_accessed=10_000_000, transcendentals=4_000_000),
    )(linear_query, linear_key, linear_value, log_decay, norm_gain.reshape(1, width),
      soft_query, soft_key, soft_value, bias)


def solution(mesh):
    in_specs = (
        P("ctx", "head"), P("ctx", "head"), P("ctx", "head"), P("head", "ctx"), P("head"),
        P("ctx", "head"), P("ctx", "head"), P("ctx", "head"), P("ctx", None), P("ctx"),
    )
    out_specs = (P(("ctx", "head"), None), P(("ctx", "head"), None))
    body = functools.partial(local, mesh.shape["ctx"], mesh.shape["head"])
    return jax.shard_map(body, mesh=mesh, in_specs=in_specs, out_specs=out_specs, check_vma=False)
```

time: 401 us -> 118 us (0.29)
  the two profiles are of different devices: /device:TPU:0 before, /device:TPU:25 now
where the time goes in v1:
time: 118 us
  Pallas kernels  110 us (93%)
  local copies, waits for them, and re-layouts  6.92 us (6%)
    pallas_call x1, Pallas kernels, local(): pl.pallas_call(functools.partial(kernel, sections, peers, heads), out_sha...  110 us
    unnamed x18, local copies, waits for them, and re-layouts  6.92 us

profile of v1, /device:TPU:25, one launch (start us, length us, event | category | flops | bytes accessed | tf_op | source)
XLA Modules:
  0.0 117.5 jit_solution(12466214746159363003)
XLA Ops:
  0.6 0.0 copy-start.6
  0.6 0.0 copy-start.5
  0.7 0.0 copy-start.3
  0.7 0.6 copy-done.6
  1.3 0.1 iota_compare_fusion
  1.4 0.1 iota_add_fusion
  1.4 0.0 copy-done.5
  1.4 0.2 and_reduce_fusion
  1.6 0.0 copy-start.4
  1.7 0.1 broadcast_bitcast_fusion
  1.8 0.0 copy-done.3
  1.8 0.6 copy-done.4
  2.4 0.0 copy-start
  2.4 1.2 %copy-done = bf16[256,2048]{1,0:T(8,128)(2,1)S(1)} copy-done((bf16[256,2048]{1,0:T(8,128)(2,1)S(1)}, bf16[256,2048]{1,0:T(8,128)(2,1)}, u32[]{:S(2)}) %copy-start) | copy-done | bytes 1048600
  3.6 0.0 copy-start.1
  3.6 1.2 %copy-done.1 = bf16[256,2048]{1,0:T(8,128)(2,1)S(1)} copy-done((bf16[256,2048]{1,0:T(8,128)(2,1)S(1)}, bf16[256,2048]{1,0:T(8,128)(2,1)}, u32[]{:S(2)}) %copy-start.1) | copy-done | bytes 1048600
  4.8 0.0 copy-start.2
  4.8 1.2 %copy-done.2 = bf16[256,2048]{1,0:T(8,128)(2,1)S(1)} copy-done((bf16[256,2048]{1,0:T(8,128)(2,1)S(1)}, bf16[256,2048]{1,0:T(8,128)(2,1)}, u32[]{:S(2)}) %copy-start.2) | copy-done | bytes 1048600
  6.0 109.5 %shard_map.113 = (bf16[64,8192]{1,0:T(8,128)(2,1)S(1)}, bf16[64,8192]{1,0:T(8,128)(2,1)S(1)}) custom-call(bf16[256,2048]{1,0:T(8,128)(2,1)S(1)} %copy-done, bf16[256,2048]{1,0:T(8,128)(2,1)S(1)} %copy-done.1, bf16[256,2048]{1,0:T(8,128)(2,1)S(1)} %copy-done.2, f32[16,256]{1,0:T(8,128)S(1)} %copy-done.3, f32[1,2048]{1,0:T(1,128)S(1)} %bitcast.7, ...), custom_call_target="tpu_custom_call" | custom-call | flops 2400000000 | bytes 10000000 | tf_op jit(solution)/shard_map/pallas_call | solution.py:303
  115.6 1.0 copy.17
  116.5 1.0 copy.18
  (3 shorter events, 0.0 us)
Async XLA Ops:
  0.6 0.7 copy-start.6
  0.6 0.8 copy-start.5
  0.7 1.1 copy-start.3
  1.6 0.7 copy-start.4
  2.4 1.2 %copy-start = (bf16[256,2048]{1,0:T(8,128)(2,1)S(1)}, bf16[256,2048]{1,0:T(8,128)(2,1)}, u32[]{:S(2)}) copy-start(bf16[256,2048]{1,0:T(8,128)(2,1)} %lq.1) | copy-start | bytes 3145732
  3.6 1.2 %copy-start.1 = (bf16[256,2048]{1,0:T(8,128)(2,1)S(1)}, bf16[256,2048]{1,0:T(8,128)(2,1)}, u32[]{:S(2)}) copy-start(bf16[256,2048]{1,0:T(8,128)(2,1)} %lk.1) | copy-start | bytes 3145732
  4.8 1.2 %copy-start.2 = (bf16[256,2048]{1,0:T(8,128)(2,1)S(1)}, bf16[256,2048]{1,0:T(8,128)(2,1)}, u32[]{:S(2)}) copy-start(bf16[256,2048]{1,0:T(8,128)(2,1)} %lv.1) | copy-start | bytes 3145732

commit v2 on v1

--- a/solution.py
+++ b/solution.py
@@ -12,6 +12,7 @@
 HD = 128
 REACH = 4
 PER_GROUP = 2
+AHEAD = 3
 EPS = 1e-06
 OFF = -1e30
 F32 = jnp.float32
@@ -26,13 +27,14 @@
 
 
 def kernel(sections, peers, heads,
-           lq, lk, lv, ld, gain, sq, sk, sv, bias,
+           lq_hbm, lk_hbm, lv_hbm, ld, gain, sq_hbm, sk_hbm, sv_hbm, bias,
            out_lin, out_soft,
-           ak, av, bk, bv, lstage, sstage, cc, g0s, g1s, exd, exp_, l1, fown, fsend, frecv, xsend, xrecv, inc,
+           lq, lk, lv, sq, sk, sv, ak, av, bk, bv, lstage, sstage,
+           cc, last, exd, exp_, fown, fsend, frecv, xsend, xrecv, inc, load,
            a_send, a_recv, b_send, b_recv, d_send, d_recv, f_send, f_recv, x_send, x_recv, o_send, o_recv, o_local):
     groups = heads // PER_GROUP
     wide = PER_GROUP * HD
-    length = lq.shape[0]
+    length = lq_hbm.shape[0]
     rows = length // peers
     c, h = lax.axis_index("ctx"), lax.axis_index("head")
     odd = lax.rem(c, 2)
@@ -55,7 +57,7 @@
 
     def copies_a(g):
         return [remote(src.at[:, cols(g)], dst.at[:, cols(g)], a_send.at[n, g], a_recv.at[n, g], {"ctx": after})
-                for n, (src, dst) in enumerate(((sk, ak), (sv, av)))]
+                for n, (src, dst) in enumerate(((sk_hbm, ak), (sv_hbm, av)))]
 
     def copies_b(g, sources):
         return [remote(src.at[:, cols(g)], dst.at[:, cols(g)], b_send.at[n, g], b_recv.at[n, g], {"ctx": partner})
@@ -88,6 +90,11 @@
         return pltpu.make_async_copy(stage.at[pl.ds(pl.multiple_of(h * rows, rows), rows), cols(g)],
                                      out.at[:, out_cols(g)], o_local.at[n, g])
 
+    loads = [pltpu.make_async_copy(src, dst, load.at[n]) for n, (src, dst) in enumerate(
+        ((lk_hbm, lk), (lv_hbm, lv), (lq_hbm, lq), (sq_hbm, sq), (sk_hbm, sk), (sv_hbm, sv)))]
+    for copy in loads:
+        copy.start()
+
     barrier = pltpu.get_barrier_semaphore()
     pl.semaphore_signal(barrier, inc=1, device_id={"ctx": partner}, device_id_type=MESH)
     for k in range(1, peers):
@@ -103,7 +110,7 @@
 
     pl.semaphore_wait(barrier, peers + has_after.astype(jnp.int32) + has_before.astype(jnp.int32))
 
-    def start_kv(g, carry):
+    def start_kv(g):
         @pl.when(has_after)
         def _():
             for copy in copies_a(g):
@@ -111,42 +118,39 @@
 
         @pl.when(odd == 0)
         def _():
-            for copy in copies_b(g, (sk, sv)):
+            for copy in copies_b(g, (sk_hbm, sv_hbm)):
                 copy.start()
-        return carry
-
-    lax.fori_loop(0, groups, start_kv, 0)
+
+    for g in range(AHEAD):
+        start_kv(g)
 
     lane = lax.broadcasted_iota(jnp.int32, (heads, length), 1)
     total = ld[...]
-    for shift in (1, 2, 4, 8, 16, 32, 64):
-        total = total + jnp.where(lax.rem(lane, BLK) >= shift, pltpu.roll(total, shift, 1), 0.0)
-    first = jnp.broadcast_to(total[:, BLK - 1:BLK], (heads, HD))
-    second = jnp.broadcast_to(total[:, 2 * BLK - 1:2 * BLK], (heads, HD))
-    whole = jnp.exp(first + second)
+    shift = 1
+    while shift < length:
+        total = total + jnp.where(lane >= shift, pltpu.roll(total, shift, 1), 0.0)
+        shift *= 2
+    ends = jnp.broadcast_to(total[:, length - 1:], (heads, HD))
+    whole = jnp.exp(ends)
     for i in range(heads):
         cc[i] = total[i:i + 1]
-        g0s[i] = first[i:i + 1]
-        g1s[i] = second[i:i + 1]
+        last[i] = ends[i:i + 1]
         exd[i] = jnp.broadcast_to(whole[i:i + 1], (8, HD))
     copy_d.start()
 
-    def columns_of(i, b):
-        along = jnp.broadcast_to(cc[i, :, pl.ds(b * BLK, BLK)], (BLK, BLK))
-        return along, along.T
+    def columns_of(i):
+        along = [jnp.broadcast_to(cc[i, :, pl.ds(b * BLK, BLK)], (BLK, BLK)) for b in range(2)]
+        return along, [part.T for part in along]
+
+    for n in (0, 1):
+        loads[n].wait()
 
     def states(g, carry):
         for n in range(PER_GROUP):
             i = g * PER_GROUP + n
-            ends = (g0s[i], g1s[i])
-            update = []
-            for b in range(2):
-                along, down = columns_of(i, b)
-                part = pl.ds(b * BLK, BLK)
-                kc = (lk[part, hcols(i)].astype(F32) * jnp.exp(ends[b] - down)).astype(BF16)
-                update.append(lax.dot_general(kc, lv[part, hcols(i)], TN, preferred_element_type=F32))
-            final = jnp.exp(ends[1]) * update[0] + update[1]
-            l1[i] = update[0].astype(BF16)
+            down = jnp.concatenate(columns_of(i)[1], axis=0)
+            kc = (lk[:, hcols(i)].astype(F32) * jnp.exp(last[i] - down)).astype(BF16)
+            final = lax.dot_general(kc, lv[:, hcols(i)], TN, preferred_element_type=F32)
             fown[i] = final
             fsend[i] = final.astype(BF16)
         copy_f(g).start()
@@ -166,9 +170,11 @@
         bv[...] = jnp.zeros_like(bv)
 
     copy_d.wait()
+    for n in range(2, 6):
+        loads[n].wait()
     r_iota = lax.broadcasted_iota(jnp.int32, (BLK, BLK), 0)
     c_iota = lax.broadcasted_iota(jnp.int32, (BLK, BLK), 1)
-    scale = 1.0 / math.sqrt(HD)
+    scale = math.log2(math.e) / math.sqrt(HD)
 
     def forward(g):
         @pl.when(has_before)
@@ -204,47 +210,56 @@
     def softmax(g):
         @pl.when(has_b)
         def _():
-            for copy in copies_b(g, (sk, sv)):
+            for copy in copies_b(g, (sk_hbm, sv_hbm)):
                 copy.wait_recv()
 
         causal = c_iota <= r_iota
-        for n in range(PER_GROUP):
-            i = g * PER_GROUP + n
+        mine = [g * PER_GROUP + n for n in range(PER_GROUP)]
+        scores = []
+        for i in mine:
             kw = jnp.concatenate([ak[:, hcols(i)], bk[:, hcols(i)], sk[:, hcols(i)]], axis=0)
-            vw = jnp.concatenate([av[:, hcols(i)], bv[:, hcols(i)], sv[:, hcols(i)]], axis=0)
+            scores.append(lax.dot_general(sq[:, hcols(i)], kw, NT, preferred_element_type=F32))
+        weights, sums = [], []
+        none = jnp.zeros((BLK, BLK), BF16)
+        for whole_s in scores:
+            parts, inverse = [], []
             for b in range(2):
-                part = pl.ds(b * BLK, BLK)
-                span = slice(b * BLK, b * BLK + (REACH + 1) * BLK)
-                s = lax.dot_general(sq[part, hcols(i)], kw[span], NT, preferred_element_type=F32) * scale
+                s = whole_s[b * BLK:(b + 1) * BLK, b * BLK:(b + REACH + 1) * BLK] * scale
                 s = jnp.concatenate([s[:, :REACH * BLK] + bias[b:b + 1, :],
                                      jnp.where(causal, s[:, REACH * BLK:], OFF)], axis=1)
-                p = jnp.exp(s - jnp.max(s, axis=1, keepdims=True))
-                w = (p * (1.0 / jnp.sum(p, axis=1, keepdims=True))).astype(BF16)
-                sstage[part, hcols(i)] = dot(w, vw[span]).astype(BF16)
+                p = jnp.exp2(s - jnp.max(s, axis=1, keepdims=True))
+                inverse.append(1.0 / jnp.sum(p, axis=1, keepdims=True))
+                p = p.astype(BF16)
+                parts.append(jnp.concatenate([p, none] if b == 0 else [none, p], axis=1))
+            weights.append(jnp.concatenate(parts, axis=0))
+            sums.append(jnp.concatenate(inverse, axis=0))
+        for i, w, inverse in zip(mine, weights, sums):
+            vw = jnp.concatenate([av[:, hcols(i)], bv[:, hcols(i)], sv[:, hcols(i)]], axis=0)
+            sstage[:, hcols(i)] = (dot(w, vw) * inverse).astype(BF16)
         for copy in copies_out(1, sstage, out_soft, g):
             copy.start()
         copy_local(1, sstage, out_soft, g).start()
 
     def linear(g):
         causal = c_iota <= r_iota
-        for n in range(PER_GROUP):
-            i = g * PER_GROUP + n
-            incoming = inc[i]
-            for b in range(2):
-                part = pl.ds(b * BLK, BLK)
-                along, down = columns_of(i, b)
-                q, k, v = lq[part, hcols(i)], lk[part, hcols(i)], lv[part, hcols(i)]
-                s = lax.dot_general(q, k, NT, preferred_element_type=F32)
-                s = s * jnp.where(causal, jnp.exp(jnp.minimum(down - along, 0.0)), 0.0)
-                raw = dot(s.astype(BF16), v)
-                wide_q = q.astype(F32)
-                if b == 0:
-                    raw += dot((wide_q * jnp.exp(down)).astype(BF16), incoming)
-                else:
-                    raw += dot((wide_q * jnp.exp(down)).astype(BF16), l1[i])
-                    raw += dot((wide_q * jnp.exp(down + g0s[i])).astype(BF16), incoming)
-                square = jnp.mean(raw * raw, axis=1, keepdims=True)
-                lstage[part, hcols(i)] = (raw * lax.rsqrt(square + EPS) * gain[:, hcols(i)]).astype(BF16)
+        mine = [g * PER_GROUP + n for n in range(PER_GROUP)]
+        none = jnp.zeros((BLK, BLK), BF16)
+        scores = [lax.dot_general(lq[:, hcols(i)], lk[:, hcols(i)], NT, preferred_element_type=F32) for i in mine]
+        left = []
+        for i, s in zip(mine, scores):
+            along, down = columns_of(i)
+            top = s[:BLK, :BLK] * jnp.where(causal, jnp.exp(down[0] - along[0]), 0.0)
+            across = s[BLK:, :BLK] * jnp.exp(down[1] - along[0])
+            low = s[BLK:, BLK:] * jnp.where(causal, jnp.exp(down[1] - along[1]), 0.0)
+            decayed = (lq[:, hcols(i)].astype(F32) * jnp.exp(jnp.concatenate(down, axis=0))).astype(BF16)
+            left.append(jnp.concatenate([
+                jnp.concatenate([top.astype(BF16), none], axis=1),
+                jnp.concatenate([across.astype(BF16), low.astype(BF16)], axis=1)], axis=0))
+            left[-1] = jnp.concatenate([left[-1], decayed], axis=1)
+        for i, p in zip(mine, left):
+            raw = dot(p, jnp.concatenate([lv[:, hcols(i)], inc[i]], axis=0))
+            square = jnp.mean(raw * raw, axis=1, keepdims=True)
+            lstage[:, hcols(i)] = (raw * lax.rsqrt(square + EPS) * gain[:, hcols(i)]).astype(BF16)
         for copy in copies_out(0, lstage, out_lin, g):
             copy.start()
         copy_local(0, lstage, out_lin, g).start()
@@ -254,11 +269,15 @@
     def main(g, carry):
         chain(g)
 
+        @pl.when(g + AHEAD < groups)
+        def _():
+            start_kv(g + AHEAD)
+        linear(g)
+
         @pl.when(g + 1 < groups)
         def _():
             forward(g + 1)
         softmax(g)
-        linear(g)
         return carry
 
     lax.fori_loop(0, groups, main, 0)
@@ -272,7 +291,7 @@
 
         @pl.when(sends_b)
         def _():
-            for copy in copies_b(g, (sk, sv)):
+            for copy in copies_b(g, (sk_hbm, sv_hbm)):
                 copy.wait_send()
         copy_f(g).wait_send()
         for n, (stage, out) in enumerate(((lstage, out_lin), (sstage, out_soft))):
@@ -296,34 +315,32 @@
     seen = jnp.any(used[:, None, :] & (block_index[:, None, :] == named[:, :, None]), axis=2)
     bias = jnp.repeat(jnp.where(seen, 0.0, OFF).astype(F32), BLK, axis=1)
     carried = BF16 if sections <= 8 else F32
-    vmem = pl.BlockSpec(memory_space=pltpu.VMEM)
+    vmem, hbm = pl.BlockSpec(memory_space=pltpu.VMEM), pl.BlockSpec(memory_space=pl.ANY)
     rows = length // peers
     state = (heads, HD, HD)
     dma = pltpu.SemaphoreType.DMA
     return pl.pallas_call(
         functools.partial(kernel, sections, peers, heads),
         out_shape=[jax.ShapeDtypeStruct((rows, width * peers), BF16)] * 2,
-        in_specs=[vmem] * 9,
-        out_specs=[pl.BlockSpec(memory_space=pl.ANY)] * 2,
-        scratch_shapes=[pltpu.VMEM((length, width), BF16)] * 6 + [
+        in_specs=[hbm, hbm, hbm, vmem, vmem, hbm, hbm, hbm, vmem],
+        out_specs=[hbm] * 2,
+        scratch_shapes=[pltpu.VMEM((length, width), BF16)] * 12 + [
             pltpu.VMEM((heads, 1, length), F32),
-            pltpu.VMEM((heads, 1, HD), F32),
             pltpu.VMEM((heads, 1, HD), F32),
             pltpu.VMEM((heads, 8, HD), F32),
             pltpu.VMEM((heads, 8, HD), F32),
-            pltpu.VMEM(state, BF16),
             pltpu.VMEM(state, F32),
             pltpu.VMEM(state, BF16),
             pltpu.VMEM(state, BF16),
             pltpu.VMEM(state, carried),
             pltpu.VMEM(state, carried),
             pltpu.VMEM(state, BF16),
-            dma((2, groups)), dma((2, groups)), dma((2, groups)), dma((2, groups)),
+            dma((6,)), dma((2, groups)), dma((2, groups)), dma((2, groups)), dma((2, groups)),
             dma, dma, dma((groups,)), dma((groups,)), dma((groups,)), dma((groups,)),
             dma((2, groups, peers - 1)), dma((2, groups, peers - 1)), dma((2, groups)),
         ],
         compiler_params=pltpu.CompilerParams(
-            collective_id=0, has_side_effects=True, vmem_limit_bytes=48 * 1024 * 1024),
+            collective_id=0, has_side_effects=True, vmem_limit_bytes=60 * 1024 * 1024),
         cost_estimate=pl.CostEstimate(flops=2_400_000_000, bytes_accessed=10_000_000, transcendentals=4_000_000),
     )(linear_query, linear_key, linear_value, log_decay, norm_gain.reshape(1, width),
       soft_query, soft_key, soft_value, bias)

time: 118 us -> 92.9 us (0.79)
  Pallas kernels: 110 us -> 86.3 us
  local copies, waits for them, and re-layouts: 6.92 us -> 5.26 us
    pallas_call x1, Pallas kernels: 110 us -> 86.3 us  [local(): pl.pallas_call(functools.partial(kernel, sections, peers, heads), out_sha...]
    unnamed x18 -> x10, local copies, waits for them, and re-layouts: 6.92 us -> 5.26 us
where the time goes in v2:
time: 92.9 us; the launch traced here: 92.6 us
  Pallas kernels  86.3 us (93%)
  local copies, waits for them, and re-layouts  5.26 us (6%)
    pallas_call x1, Pallas kernels, local(): pl.pallas_call(functools.partial(kernel, sections, peers, heads), out_sha...  86.3 us
    unnamed x10, local copies, waits for them, and re-layouts  5.26 us

profile of v2, /device:TPU:25, one launch (start us, length us, event | category | flops | bytes accessed | tf_op | source)
XLA Modules:
  0.0 92.6 jit_solution(13509788257131828058)
XLA Ops:
  0.6 0.0 copy-start.2
  0.7 0.6 copy-done.2
  1.3 0.1 iota_compare_fusion
  1.4 0.0 copy-start.1
  1.4 0.1 iota_add_fusion
  1.4 0.6 copy-done.1
  2.1 0.2 and_reduce_fusion
  2.3 0.1 broadcast_bitcast_fusion
  2.4 0.6 copy.14
  3.0 86.3 %shard_map.113 = (bf16[64,8192]{1,0:T(8,128)(2,1)}, bf16[64,8192]{1,0:T(8,128)(2,1)}) custom-call(bf16[256,2048]{1,0:T(8,128)(2,1)} %lq_hbm.1, bf16[256,2048]{1,0:T(8,128)(2,1)} %lk_hbm.1, bf16[256,2048]{1,0:T(8,128)(2,1)} %lv_hbm.1, f32[16,256]{1,0:T(8,128)} %ld.1, f32[1,2048]{1,0:T(1,128)} %bitcast.7, bf16[256,2048]{1,0:T(8,128)(2,1)} %sq_hbm.1, ...), custom_call_target="tpu_custom_call" | custom-call | flops 2400000000 | bytes 10000000 | tf_op jit(solution)/shard_map/pallas_call | solution.py:322
  89.3 0.0 copy-start
  89.3 2.4 %copy.17 = bf16[64,8192]{1,0:T(8,128)(2,1)} copy(bf16[64,8192]{1,0:T(8,128)(2,1)} %get-tuple-element.4) | data formatting | bytes 2097152
  91.7 0.0 copy-done
  91.7 1.0 %copy.18 = bf16[64,8192]{1,0:T(8,128)(2,1)} copy(bf16[64,8192]{1,0:T(8,128)(2,1)S(1)} %copy-done) | data formatting | bytes 2097152
  (2 shorter events, 0.0 us)
Async XLA Ops:
  0.6 0.7 copy-start.2
  1.4 0.7 copy-start.1
  89.3 2.4 %copy-start = (bf16[64,8192]{1,0:T(8,128)(2,1)S(1)}, bf16[64,8192]{1,0:T(8,128)(2,1)}, u32[]{:S(2)}) copy-start(bf16[64,8192]{1,0:T(8,128)(2,1)} %get-tuple-element.5) | copy-start | bytes 3145732

commit v3 on v2

--- a/solution.py
+++ b/solution.py
@@ -12,7 +12,8 @@
 HD = 128
 REACH = 4
 PER_GROUP = 2
-AHEAD = 3
+AHEAD = 4
+RATE = 2
 EPS = 1e-06
 OFF = -1e30
 F32 = jnp.float32
@@ -27,9 +28,9 @@
 
 
 def kernel(sections, peers, heads,
-           lq_hbm, lk_hbm, lv_hbm, ld, gain, sq_hbm, sk_hbm, sv_hbm, bias,
+           lq_hbm, lk_hbm, lv_hbm, ld_hbm, gain_hbm, sq_hbm, sk_hbm, sv_hbm, index, count,
            out_lin, out_soft,
-           lq, lk, lv, sq, sk, sv, ak, av, bk, bv, lstage, sstage,
+           lq, lk, lv, sq, sk, sv, ak, av, bk, bv, lstage, sstage, ld, gain, bias,
            cc, last, exd, exp_, fown, fsend, frecv, xsend, xrecv, inc, load,
            a_send, a_recv, b_send, b_recv, d_send, d_recv, f_send, f_recv, x_send, x_recv, o_send, o_recv, o_local):
     groups = heads // PER_GROUP
@@ -91,9 +92,10 @@
                                      out.at[:, out_cols(g)], o_local.at[n, g])
 
     loads = [pltpu.make_async_copy(src, dst, load.at[n]) for n, (src, dst) in enumerate(
-        ((lk_hbm, lk), (lv_hbm, lv), (lq_hbm, lq), (sq_hbm, sq), (sk_hbm, sk), (sv_hbm, sv)))]
-    for copy in loads:
-        copy.start()
+        ((lk_hbm, lk), (lv_hbm, lv), (lq_hbm, lq), (sq_hbm, sq), (sk_hbm, sk), (sv_hbm, sv),
+         (ld_hbm, ld), (gain_hbm, gain)))]
+    for n in (6, 7, 0, 1, 2, 3, 4, 5):
+        loads[n].start()
 
     barrier = pltpu.get_barrier_semaphore()
     pl.semaphore_signal(barrier, inc=1, device_id={"ctx": partner}, device_id_type=MESH)
@@ -121,9 +123,9 @@
             for copy in copies_b(g, (sk_hbm, sv_hbm)):
                 copy.start()
 
-    for g in range(AHEAD):
-        start_kv(g)
-
+    start_kv(0)
+    for n in (6, 7):
+        loads[n].wait()
     lane = lax.broadcasted_iota(jnp.int32, (heads, length), 1)
     total = ld[...]
     shift = 1
@@ -154,6 +156,10 @@
             fown[i] = final
             fsend[i] = final.astype(BF16)
         copy_f(g).start()
+
+        @pl.when(g + 1 < AHEAD)
+        def _():
+            start_kv(g + 1)
         return carry
 
     lax.fori_loop(0, groups, states, 0)
@@ -170,6 +176,14 @@
         bv[...] = jnp.zeros_like(bv)
 
     copy_d.wait()
+    here = length // BLK
+    for b in range(here):
+        tiles = []
+        for w in range(REACH):
+            block = here * c + b - REACH + w
+            seen = [jnp.logical_and(slot < count[b], index[b, slot] == block) for slot in range(index.shape[1])]
+            tiles.append(jnp.full((1, BLK), jnp.where(functools.reduce(jnp.logical_or, seen), 0.0, OFF), F32))
+        bias[b:b + 1, :] = jnp.concatenate(tiles, axis=1)
     for n in range(2, 6):
         loads[n].wait()
     r_iota = lax.broadcasted_iota(jnp.int32, (BLK, BLK), 0)
@@ -266,21 +280,35 @@
 
     forward(0)
 
+    stage = (c - odd) // 2
+
     def main(g, carry):
-        chain(g)
-
         @pl.when(g + AHEAD < groups)
         def _():
             start_kv(g + AHEAD)
-        linear(g)
 
         @pl.when(g + 1 < groups)
         def _():
             forward(g + 1)
-        softmax(g)
+
+        ready = RATE * (g - stage)
+        for n in range(RATE):
+            @pl.when(jnp.logical_and(ready + n >= 0, ready + n < groups))
+            def _():
+                chain(ready + n)
+
+        @pl.when(g < groups)
+        def _():
+            softmax(g)
+
+        for n in range(RATE):
+            @pl.when(jnp.logical_and(ready + n >= 0, ready + n < groups))
+            def _():
+                linear(ready + n)
         return carry
 
-    lax.fori_loop(0, groups, main, 0)
+    steps = max(groups, -(-groups // RATE) + (sections + 1) // 2 - 1)
+    lax.fori_loop(0, steps, main, 0)
 
     def finish(g, carry):
         @pl.when(has_after)
@@ -308,23 +336,20 @@
     heads, length = log_decay.shape
     width = linear_query.shape[1]
     groups = heads // PER_GROUP
-    here = length // BLK
-    own = lax.axis_index("ctx") * here + jnp.arange(here, dtype=jnp.int32)
-    named = own[:, None] - REACH + jnp.arange(REACH, dtype=jnp.int32)[None, :]
-    used = jnp.arange(block_index.shape[1], dtype=jnp.int32)[None, :] < block_count[:, None]
-    seen = jnp.any(used[:, None, :] & (block_index[:, None, :] == named[:, :, None]), axis=2)
-    bias = jnp.repeat(jnp.where(seen, 0.0, OFF).astype(F32), BLK, axis=1)
     carried = BF16 if sections <= 8 else F32
-    vmem, hbm = pl.BlockSpec(memory_space=pltpu.VMEM), pl.BlockSpec(memory_space=pl.ANY)
+    smem, hbm = pl.BlockSpec(memory_space=pltpu.SMEM), pl.BlockSpec(memory_space=pl.ANY)
     rows = length // peers
     state = (heads, HD, HD)
     dma = pltpu.SemaphoreType.DMA
     return pl.pallas_call(
         functools.partial(kernel, sections, peers, heads),
         out_shape=[jax.ShapeDtypeStruct((rows, width * peers), BF16)] * 2,
-        in_specs=[hbm, hbm, hbm, vmem, vmem, hbm, hbm, hbm, vmem],
+        in_specs=[hbm] * 8 + [smem] * 2,
         out_specs=[hbm] * 2,
         scratch_shapes=[pltpu.VMEM((length, width), BF16)] * 12 + [
+            pltpu.VMEM((heads, length), F32),
+            pltpu.VMEM((1, width), F32),
+            pltpu.VMEM((length // BLK, REACH * BLK), F32),
             pltpu.VMEM((heads, 1, length), F32),
             pltpu.VMEM((heads, 1, HD), F32),
             pltpu.VMEM((heads, 8, HD), F32),
@@ -335,7 +360,7 @@
             pltpu.VMEM(state, carried),
             pltpu.VMEM(state, carried),
             pltpu.VMEM(state, BF16),
-            dma((6,)), dma((2, groups)), dma((2, groups)), dma((2, groups)), dma((2, groups)),
+            dma((8,)), dma((2, groups)), dma((2, groups)), dma((2, groups)), dma((2, groups)),
             dma, dma, dma((groups,)), dma((groups,)), dma((groups,)), dma((groups,)),
             dma((2, groups, peers - 1)), dma((2, groups, peers - 1)), dma((2, groups)),
         ],
@@ -343,7 +368,7 @@
             collective_id=0, has_side_effects=True, vmem_limit_bytes=60 * 1024 * 1024),
         cost_estimate=pl.CostEstimate(flops=2_400_000_000, bytes_accessed=10_000_000, transcendentals=4_000_000),
     )(linear_query, linear_key, linear_value, log_decay, norm_gain.reshape(1, width),
-      soft_query, soft_key, soft_value, bias)
+      soft_query, soft_key, soft_value, block_index, block_count)
 
 
 def solution(mesh):

time: 92.9 us -> 85.4 us (0.919)
  the two profiles are of different devices: /device:TPU:25 before, /device:TPU:11 now
where the time goes in v3:
time: 85.4 us; the launch traced here: 85.3 us
  Pallas kernels  81.3 us (95%)
  local copies, waits for them, and re-layouts  3.32 us (4%)
    pallas_call x1, Pallas kernels, local(): pl.pallas_call(functools.partial(kernel, sections, peers, heads), out_sha...  81.3 us
    unnamed x4, local copies, waits for them, and re-layouts  3.32 us

profile of v3, /device:TPU:11, one launch (start us, length us, event | category | flops | bytes accessed | tf_op | source)
XLA Modules:
  0.0 85.3 jit_solution(13375399078675010514)
XLA Ops:
  0.6 81.3 %shard_map.113 = (bf16[64,8192]{1,0:T(8,128)(2,1)}, bf16[64,8192]{1,0:T(8,128)(2,1)}) custom-call(bf16[256,2048]{1,0:T(8,128)(2,1)} %lq_hbm.1, bf16[256,2048]{1,0:T(8,128)(2,1)} %lk_hbm.1, bf16[256,2048]{1,0:T(8,128)(2,1)} %lv_hbm.1, f32[16,256]{1,0:T(8,128)} %ld_hbm.1, f32[1,2048]{1,0:T(1,128)} %bitcast.1, bf16[256,2048]{1,0:T(8,128)(2,1)} %sq_hbm.1, ...), custom_call_target="tpu_custom_call" | custom-call | flops 2400000000 | bytes 10000000 | tf_op jit(solution)/shard_map/pallas_call | solution.py:344
  81.9 0.0 copy-start
  81.9 2.4 %copy.14 = bf16[64,8192]{1,0:T(8,128)(2,1)} copy(bf16[64,8192]{1,0:T(8,128)(2,1)} %get-tuple-element.4) | data formatting | bytes 2097152
  84.3 0.0 copy-done
  84.3 1.0 %copy.15 = bf16[64,8192]{1,0:T(8,128)(2,1)} copy(bf16[64,8192]{1,0:T(8,128)(2,1)S(1)} %copy-done) | data formatting | bytes 2097152
Async XLA Ops:
  81.9 2.4 %copy-start = (bf16[64,8192]{1,0:T(8,128)(2,1)S(1)}, bf16[64,8192]{1,0:T(8,128)(2,1)}, u32[]{:S(2)}) copy-start(bf16[64,8192]{1,0:T(8,128)(2,1)} %get-tuple-element.5) | copy-start | bytes 3145732

commit v4 on v3

--- a/solution.py
+++ b/solution.py
@@ -11,7 +11,7 @@
 BLK = 128
 HD = 128
 REACH = 4
-PER_GROUP = 2
+PER_GROUP = 1
 AHEAD = 4
 RATE = 2
 EPS = 1e-06
@@ -44,7 +44,6 @@
     after, before = lax.rem(c + 2, sections), lax.rem(c + sections - 2, sections)
     has_after, has_before = c + 2 < sections, c >= 2
     has_b = c >= 1
-    sends_b = jnp.logical_or(odd == 0, has_before)
 
     def cols(g):
         return pl.ds(pl.multiple_of(g * wide, wide), wide)
@@ -122,6 +121,17 @@
         def _():
             for copy in copies_b(g, (sk_hbm, sv_hbm)):
                 copy.start()
+
+    def sent_kv(g):
+        @pl.when(has_after)
+        def _():
+            for copy in copies_a(g):
+                copy.wait_send()
+
+        @pl.when(odd == 0)
+        def _():
+            for copy in copies_b(g, (sk_hbm, sv_hbm)):
+                copy.wait_send()
 
     start_kv(0)
     for n in (6, 7):
@@ -285,6 +295,7 @@
     def main(g, carry):
         @pl.when(g + AHEAD < groups)
         def _():
+            sent_kv(g)
             start_kv(g + AHEAD)
 
         @pl.when(g + 1 < groups)
@@ -311,15 +322,17 @@
     lax.fori_loop(0, steps, main, 0)
 
     def finish(g, carry):
+        @pl.when(g >= groups - AHEAD)
+        def _():
+            sent_kv(g)
+
         @pl.when(has_after)
         def _():
-            for copy in copies_a(g):
-                copy.wait_send()
             copy_x(g).wait_send()
 
-        @pl.when(sends_b)
-        def _():
-            for copy in copies_b(g, (sk_hbm, sv_hbm)):
+        @pl.when(jnp.logical_and(odd == 1, has_before))
+        def _():
+            for copy in copies_b(g, (ak, av)):
                 copy.wait_send()
         copy_f(g).wait_send()
         for n, (stage, out) in enumerate(((lstage, out_lin), (sstage, out_soft))):

time: 85.4 us -> 81.2 us (0.951)
  the two profiles are of different devices: /device:TPU:11 before, /device:TPU:25 now
where the time goes in v4:
time: 81.2 us; the launch traced here: 81 us
  Pallas kernels  77 us (95%)
  local copies, waits for them, and re-layouts  3.32 us (4%)
    pallas_call x1, Pallas kernels, local(): pl.pallas_call(functools.partial(kernel, sections, peers, heads), out_sha...  77 us
    unnamed x4, local copies, waits for them, and re-layouts  3.32 us

profile of v4, /device:TPU:25, one launch (start us, length us, event | category | flops | bytes accessed | tf_op | source)
XLA Modules:
  0.0 81.0 jit_solution(16892852577641643289)
XLA Ops:
  0.6 77.0 %shard_map.113 = (bf16[64,8192]{1,0:T(8,128)(2,1)}, bf16[64,8192]{1,0:T(8,128)(2,1)}) custom-call(bf16[256,2048]{1,0:T(8,128)(2,1)} %lq_hbm.1, bf16[256,2048]{1,0:T(8,128)(2,1)} %lk_hbm.1, bf16[256,2048]{1,0:T(8,128)(2,1)} %lv_hbm.1, f32[16,256]{1,0:T(8,128)} %ld_hbm.1, f32[1,2048]{1,0:T(1,128)} %bitcast.1, bf16[256,2048]{1,0:T(8,128)(2,1)} %sq_hbm.1, ...), custom_call_target="tpu_custom_call" | custom-call | flops 2400000000 | bytes 10000000 | tf_op jit(solution)/shard_map/pallas_call | solution.py:357
  77.6 0.0 copy-start
  77.7 2.4 %copy.14 = bf16[64,8192]{1,0:T(8,128)(2,1)} copy(bf16[64,8192]{1,0:T(8,128)(2,1)} %get-tuple-element.4) | data formatting | bytes 2097152
  80.0 0.0 copy-done
  80.0 1.0 %copy.15 = bf16[64,8192]{1,0:T(8,128)(2,1)} copy(bf16[64,8192]{1,0:T(8,128)(2,1)S(1)} %copy-done) | data formatting | bytes 2097152
Async XLA Ops:
  77.6 2.4 %copy-start = (bf16[64,8192]{1,0:T(8,128)(2,1)S(1)}, bf16[64,8192]{1,0:T(8,128)(2,1)}, u32[]{:S(2)}) copy-start(bf16[64,8192]{1,0:T(8,128)(2,1)} %get-tuple-element.5) | copy-start | bytes 3145732

commit v5 on v4

--- a/solution.py
+++ b/solution.py
@@ -31,7 +31,7 @@
            lq_hbm, lk_hbm, lv_hbm, ld_hbm, gain_hbm, sq_hbm, sk_hbm, sv_hbm, index, count,
            out_lin, out_soft,
            lq, lk, lv, sq, sk, sv, ak, av, bk, bv, lstage, sstage, ld, gain, bias,
-           cc, last, exd, exp_, fown, fsend, frecv, xsend, xrecv, inc, load,
+           cc, last, exd, exp_, fown, fsend, frecv, xsend, xrecv, inc, load, kv_load,
            a_send, a_recv, b_send, b_recv, d_send, d_recv, f_send, f_recv, x_send, x_recv, o_send, o_recv, o_local):
     groups = heads // PER_GROUP
     wide = PER_GROUP * HD
@@ -56,11 +56,11 @@
             src_ref=src, dst_ref=dst, send_sem=send, recv_sem=recv, device_id=where, device_id_type=MESH)
 
     def copies_a(g):
-        return [remote(src.at[:, cols(g)], dst.at[:, cols(g)], a_send.at[n, g], a_recv.at[n, g], {"ctx": after})
-                for n, (src, dst) in enumerate(((sk_hbm, ak), (sv_hbm, av)))]
+        return [remote(src.at[hd(g)], dst.at[hd(g)], a_send.at[n, g], a_recv.at[n, g], {"ctx": after})
+                for n, (src, dst) in enumerate(((sk, ak), (sv, av)))]
 
     def copies_b(g, sources):
-        return [remote(src.at[:, cols(g)], dst.at[:, cols(g)], b_send.at[n, g], b_recv.at[n, g], {"ctx": partner})
+        return [remote(src.at[hd(g)], dst.at[hd(g)], b_send.at[n, g], b_recv.at[n, g], {"ctx": partner})
                 for n, (src, dst) in enumerate(zip(sources, (bk, bv)))]
 
     def hd(g):
@@ -91,10 +91,22 @@
                                      out.at[:, out_cols(g)], o_local.at[n, g])
 
     loads = [pltpu.make_async_copy(src, dst, load.at[n]) for n, (src, dst) in enumerate(
-        ((lk_hbm, lk), (lv_hbm, lv), (lq_hbm, lq), (sq_hbm, sq), (sk_hbm, sk), (sv_hbm, sv),
+        ((lk_hbm, lk), (lv_hbm, lv), (lq_hbm, lq), (sq_hbm, sq),
          (ld_hbm, ld), (gain_hbm, gain)))]
-    for n in (6, 7, 0, 1, 2, 3, 4, 5):
+
+    def kv_loads(i):
+        return [pltpu.make_async_copy(src.at[:, hcols(i)], dst.at[i], kv_load.at[n, i])
+                for n, (src, dst) in enumerate(((sk_hbm, sk), (sv_hbm, sv)))]
+
+    def load_kv(i, carry):
+        for copy in kv_loads(i):
+            copy.start()
+        return carry
+
+    lax.fori_loop(0, AHEAD * PER_GROUP, load_kv, 0)
+    for n in (4, 5, 0, 1, 2, 3):
         loads[n].start()
+    lax.fori_loop(AHEAD * PER_GROUP, heads, load_kv, 0)
 
     barrier = pltpu.get_barrier_semaphore()
     pl.semaphore_signal(barrier, inc=1, device_id={"ctx": partner}, device_id_type=MESH)
@@ -112,6 +124,10 @@
     pl.semaphore_wait(barrier, peers + has_after.astype(jnp.int32) + has_before.astype(jnp.int32))
 
     def start_kv(g):
+        for n in range(PER_GROUP):
+            for copy in kv_loads(g * PER_GROUP + n):
+                copy.wait()
+
         @pl.when(has_after)
         def _():
             for copy in copies_a(g):
@@ -119,7 +135,7 @@
 
         @pl.when(odd == 0)
         def _():
-            for copy in copies_b(g, (sk_hbm, sv_hbm)):
+            for copy in copies_b(g, (sk, sv)):
                 copy.start()
 
     def sent_kv(g):
@@ -130,11 +146,11 @@
 
         @pl.when(odd == 0)
         def _():
-            for copy in copies_b(g, (sk_hbm, sv_hbm)):
+            for copy in copies_b(g, (sk, sv)):
                 copy.wait_send()
 
     start_kv(0)
-    for n in (6, 7):
+    for n in (4, 5):
         loads[n].wait()
     lane = lax.broadcasted_iota(jnp.int32, (heads, length), 1)
     total = ld[...]
@@ -194,7 +210,7 @@
             seen = [jnp.logical_and(slot < count[b], index[b, slot] == block) for slot in range(index.shape[1])]
             tiles.append(jnp.full((1, BLK), jnp.where(functools.reduce(jnp.logical_or, seen), 0.0, OFF), F32))
         bias[b:b + 1, :] = jnp.concatenate(tiles, axis=1)
-    for n in range(2, 6):
+    for n in (2, 3):
         loads[n].wait()
     r_iota = lax.broadcasted_iota(jnp.int32, (BLK, BLK), 0)
     c_iota = lax.broadcasted_iota(jnp.int32, (BLK, BLK), 1)
@@ -234,14 +250,14 @@
     def softmax(g):
         @pl.when(has_b)
         def _():
-            for copy in copies_b(g, (sk_hbm, sv_hbm)):
+            for copy in copies_b(g, (sk, sv)):
                 copy.wait_recv()
 
         causal = c_iota <= r_iota
         mine = [g * PER_GROUP + n for n in range(PER_GROUP)]
         scores = []
         for i in mine:
-            kw = jnp.concatenate([ak[:, hcols(i)], bk[:, hcols(i)], sk[:, hcols(i)]], axis=0)
+            kw = jnp.concatenate([ak[i], bk[i], sk[i]], axis=0)
             scores.append(lax.dot_general(sq[:, hcols(i)], kw, NT, preferred_element_type=F32))
         weights, sums = [], []
         none = jnp.zeros((BLK, BLK), BF16)
@@ -258,7 +274,7 @@
             weights.append(jnp.concatenate(parts, axis=0))
             sums.append(jnp.concatenate(inverse, axis=0))
         for i, w, inverse in zip(mine, weights, sums):
-            vw = jnp.concatenate([av[:, hcols(i)], bv[:, hcols(i)], sv[:, hcols(i)]], axis=0)
+            vw = jnp.concatenate([av[i], bv[i], sv[i]], axis=0)
             sstage[:, hcols(i)] = (dot(w, vw) * inverse).astype(BF16)
         for copy in copies_out(1, sstage, out_soft, g):
             copy.start()
@@ -359,7 +375,8 @@
         out_shape=[jax.ShapeDtypeStruct((rows, width * peers), BF16)] * 2,
         in_specs=[hbm] * 8 + [smem] * 2,
         out_specs=[hbm] * 2,
-        scratch_shapes=[pltpu.VMEM((length, width), BF16)] * 12 + [
+        scratch_shapes=[pltpu.VMEM((length, width), BF16)] * 4 + [pltpu.VMEM((heads, length, HD), BF16)] * 6 + [
+            pltpu.VMEM((length, width), BF16), pltpu.VMEM((length, width), BF16),
             pltpu.VMEM((heads, length), F32),
             pltpu.VMEM((1, width), F32),
             pltpu.VMEM((length // BLK, REACH * BLK), F32),
@@ -373,7 +390,7 @@
             pltpu.VMEM(state, carried),
             pltpu.VMEM(state, carried),
             pltpu.VMEM(state, BF16),
-            dma((8,)), dma((2, groups)), dma((2, groups)), dma((2, groups)), dma((2, groups)),
+            dma((6,)), dma((2, heads)), dma((2, groups)), dma((2, groups)), dma((2, groups)), dma((2, groups)),
             dma, dma, dma((groups,)), dma((groups,)), dma((groups,)), dma((groups,)),
             dma((2, groups, peers - 1)), dma((2, groups, peers - 1)), dma((2, groups)),
         ],

time: 81.2 us -> 81.1 us (level)
  no operation moved by 1% of the time
where the time goes in v5:
time: 81.1 us; the launch traced here: 80.9 us
  Pallas kernels  76.9 us (95%)
  local copies, waits for them, and re-layouts  3.32 us (4%)
    pallas_call x1, Pallas kernels, local(): pl.pallas_call(functools.partial(kernel, sections, peers, heads), out_sha...  76.9 us
    unnamed x4, local copies, waits for them, and re-layouts  3.32 us

profile of v5, /device:TPU:25, one launch (start us, length us, event | category | flops | bytes accessed | tf_op | source)
XLA Modules:
  0.0 80.9 jit_solution(2051336752044982599)
XLA Ops:
  0.6 76.9 %shard_map.113 = (bf16[64,8192]{1,0:T(8,128)(2,1)}, bf16[64,8192]{1,0:T(8,128)(2,1)}) custom-call(bf16[256,2048]{1,0:T(8,128)(2,1)} %lq_hbm.1, bf16[256,2048]{1,0:T(8,128)(2,1)} %lk_hbm.1, bf16[256,2048]{1,0:T(8,128)(2,1)} %lv_hbm.1, f32[16,256]{1,0:T(8,128)} %ld_hbm.1, f32[1,2048]{1,0:T(1,128)} %bitcast.1, bf16[256,2048]{1,0:T(8,128)(2,1)} %sq_hbm.1, ...), custom_call_target="tpu_custom_call" | custom-call | flops 2400000000 | bytes 10000000 | tf_op jit(solution)/shard_map/pallas_call | solution.py:373
  77.6 0.0 copy-start
  77.6 2.4 %copy.14 = bf16[64,8192]{1,0:T(8,128)(2,1)} copy(bf16[64,8192]{1,0:T(8,128)(2,1)} %get-tuple-element.4) | data formatting | bytes 2097152
  79.9 0.0 copy-done
  79.9 1.0 %copy.15 = bf16[64,8192]{1,0:T(8,128)(2,1)} copy(bf16[64,8192]{1,0:T(8,128)(2,1)S(1)} %copy-done) | data formatting | bytes 2097152
Async XLA Ops:
  77.6 2.4 %copy-start = (bf16[64,8192]{1,0:T(8,128)(2,1)S(1)}, bf16[64,8192]{1,0:T(8,128)(2,1)}, u32[]{:S(2)}) copy-start(bf16[64,8192]{1,0:T(8,128)(2,1)} %get-tuple-element.5) | copy-start | bytes 3145732
